TPU v7x, 512 devices: a whole 4x8x8 slice. The times are simulated.
512 devices in a mesh: rows: 64 (over x, y, core), probe: 8 (over z).
Axes of the slice: x: 4, y: 8, z: 8, core: 2. Of those that a mesh axis runs over, the one named last changes fastest.
Arguments:
- targets: float32 [3, 65536], P(None, 'rows'), may hold values from 0 to 1
- sources: bfloat16 [3, 8192], P(None, 'rows'), may hold values from 0 to 1
- probes: bfloat16 [256, 8192], P('probe', 'rows'), may hold values from -6 to 6
- cluster_sizes: int32 [512], P(('rows', 'probe')), may hold values from 64 to 128, as said below
- leaf_ranks: int32 [512], P(('rows', 'probe')), may hold values from 128 to 256, as said below
Outputs:
- leaf_basis: float32 [256, 2, 65536], P(None, None, ('rows', 'probe'))
- top_factor: float32 [512, 256, 256], P(('rows', 'probe'))
Inputs may be any that keep to these rules, and one draw needn't show every extreme that they name: `cluster_sizes`: some leaf uses all 128 points in every draw. `leaf_ranks`: some leaf keeps all 256 rows in every draw.
All inputs are finite; a program needn't handle non-finite values.
Results may differ from a plain program's by a relative error of at most 0.0033.
Values may be sent and summed in bfloat16 or wider, within the bound.
A program may use at most 64 MiB of HBM per device.

v0:
```python
import math
import jax
import jax.numpy as jnp
from jax import lax
from jax.sharding import PartitionSpec as P

wavenumber = 30.0
softening = 0.02


def partner_2(value, axis, apart):
    mask = 2**apart
    pairs = [(source, source ^ mask) for source in range(lax.axis_size(axis))]
    return lax.ppermute(value, axis, pairs)


def kernel_pair(source_pts, target_pts, col_total):
    diff_x = source_pts[0][:, None] - target_pts[0][None, :]
    diff_y = source_pts[1][:, None] - target_pts[1][None, :]
    diff_z = source_pts[2][:, None] - target_pts[2][None, :]
    distance = jnp.sqrt(diff_x * diff_x + diff_y * diff_y + diff_z * diff_z + softening * softening)
    amplitude = 1.0 / (distance * jnp.sqrt(jnp.float32(col_total)))
    kernel_cos = (amplitude * jnp.cos(wavenumber * distance)).astype(jnp.bfloat16)
    kernel_sin = (amplitude * jnp.sin(wavenumber * distance)).astype(jnp.bfloat16)
    return (kernel_cos, kernel_sin)


def sample_block(probe_piece, source_piece, target_pts, col_total):
    columns = probe_piece.shape[1]
    block_cols = math.gcd(columns, 256)
    block_count = columns // block_cols
    probe_parts = probe_piece.reshape(probe_piece.shape[0], block_count, block_cols).transpose(
        1, 0, 2
    )
    source_parts = source_piece.reshape(3, block_count, block_cols).transpose(1, 0, 2)

    def advance(running, pieces):
        probe_part, source_part = pieces
        kernel_cos, kernel_sin = kernel_pair(source_part.astype(jnp.float32), target_pts, col_total)
        part_cos = jnp.dot(probe_part, kernel_cos, preferred_element_type=jnp.float32)
        part_sin = jnp.dot(probe_part, kernel_sin, preferred_element_type=jnp.float32)
        return (running + jnp.stack([part_cos, part_sin]), None)

    starting = jnp.zeros((2, probe_piece.shape[0], target_pts.shape[1]), jnp.float32)
    result, _ = lax.scan(advance, starting, (probe_parts, source_parts))
    return result


def make_adder(target_pts, col_total):

    def add_columns(running, pieces, offset_col):
        return sample_block(pieces[0], pieces[1], target_pts, col_total)

    return add_columns


def cholesky_basis(matrix, nprobe_total):
    gram_matrix = jnp.dot(matrix, matrix.T, precision=lax.Precision.HIGHEST)
    shift_value = jnp.trace(gram_matrix) / nprobe_total
    factor = jnp.linalg.cholesky(
        gram_matrix + shift_value * jnp.eye(nprobe_total, dtype=matrix.dtype)
    )
    return jax.scipy.linalg.solve_triangular(factor, matrix, lower=True)


def per_device(targets, sources, probes, cluster_sizes, leaf_ranks):
    col_total = sources.shape[1] * lax.axis_size("rows")
    nprobe_total = probes.shape[0] * lax.axis_size("probe")
    leaf_rows = targets.shape[1] // lax.axis_size("probe")
    own_targets = lax.dynamic_slice_in_dim(
        targets, lax.axis_index("probe") * leaf_rows, leaf_rows, 1
    )
    all_probes = lax.all_gather(probes, "probe", axis=0, tiled=True)
    adder = make_adder(own_targets, col_total)
    starting = jnp.zeros((2, nprobe_total, leaf_rows), jnp.float32)
    samples = adder(
        starting,
        (
            lax.all_gather(all_probes, "rows", axis=1, tiled=True),
            lax.all_gather(sources, "rows", axis=1, tiled=True),
        ),
        jnp.int32(0),
    )
    kept_rows = (jnp.arange(leaf_rows) < cluster_sizes[0]).astype(jnp.float32)
    matrix = jnp.concatenate([samples[0] * kept_rows, samples[1] * kept_rows], axis=1)
    basis_rows = cholesky_basis(matrix, nprobe_total)
    rank_rows = (jnp.arange(nprobe_total) < leaf_ranks[0]).astype(jnp.float32)
    basis_rows = basis_rows * rank_rows[:, None]
    projected = jnp.dot(matrix, basis_rows.T, precision=lax.Precision.HIGHEST)
    row_index = lax.axis_index("rows")
    for tree_bit in range(2):
        partner = partner_2(projected, "rows", tree_bit)
        is_left = row_index >> tree_bit & 1 == 0
        left_part = jnp.where(is_left, projected, partner)
        right_part = jnp.where(is_left, partner, projected)
        stacked = jnp.concatenate([left_part, right_part], axis=1)
        node_basis = cholesky_basis(stacked, nprobe_total)
        projected = jnp.dot(stacked, node_basis.T, precision=lax.Precision.HIGHEST)
    return (basis_rows.reshape(nprobe_total, 2, leaf_rows), projected[None])


def solution(mesh):
    return jax.shard_map(
        per_device,
        mesh=mesh,
        in_specs=(
            P(None, "rows"),
            P(None, "rows"),
            P("probe", "rows"),
            P(("rows", "probe")),
            P(("rows", "probe")),
        ),
        out_specs=(P(None, None, ("rows", "probe")), P(("rows", "probe"), None, None)),
        check_vma=False,
    )
```

profile of v0, /device:TPU:1, one launch (start us, length us, event | category | flops | bytes accessed | tf_op | source)
XLA Modules:
  0.0 452.6 jit_solution(17370533172197070458)
XLA Ops:
  7.2 25.9 %all_gather.9 = bf16[256,128]{1,0:T(8,128)(2,1)S(1)} all-gather(bf16[32,128]{1,0:T(8,128)(2,1)} %param.12), channel_id=1, replica_groups=mesh['rows'=64,'probe'=8] {'probe'}, dimensions={0}, use_global_device_ids=true | all-gather | bytes 73728 | tf_op jit(solution)/shard_map/all_gather | solution.py:73
  35.2 46.2 %all_gather.11 = bf16[3,8192]{1,0:T(4,128)(2,1)S(1)} all-gather(bf16[3,128]{1,0:T(4,128)(2,1)} %param.11), channel_id=1, replica_groups=mesh['rows'=64,'probe'=8] {'rows'}, dimensions={1}, use_global_device_ids=true | all-gather | bytes 49920 | tf_op jit(solution)/shard_map/all_gather | solution.py:80
  81.4 41.8 %all-gather.2.cloned.1.call-done = bf16[256,8192]{0,1:T(8,128)(2,1)} async-done(((bf16[256,128]{0,1:T(8,128)(2,1)}), bf16[256,8192]{0,1:T(8,128)(2,1)}) %all-gather.2.cloned.1.call-update) | async-done | bytes 4194320 | tf_op jit(solution)/shard_map/all_gather | solution.py:79
  123.2 113.8 %while.17 = (s32[]{:T(128)}, f32[2,256,128]{2,1,0:T(8,128)S(1)}, bf16[32,256,256]{1,2,0:T(8,128)(2,1)}, bf16[32,3,256]{2,1,0:T(4,128)(2,1)S(1)}, f32[3,128]{1,0:T(4,128)S(1)}, /*index=5*/s32[]{:T(128)}, s32[]{:T(128)}) while((s32[]{:T(128)}, f32[2,256,128]{2,1,0:T(8,128)S(1)}, bf16[32,256,256]{1,2,0:T(8,128)(2,1)}, ...), condition=%wide.region_1.2_spmd.clone, body=%wide.region_0.1_spmd.clone.sunk | while | flops 34669312 | bytes 1334875 | solution.py:45
  124.9 1.7 convolution_bitcast_fusion.5
  126.8 1.7 convolution_bitcast_fusion.6
  128.5 1.7 convolution_bitcast_fusion.5
  132.0 1.7 convolution_bitcast_fusion.5
  135.6 1.7 convolution_bitcast_fusion.5
  137.4 1.7 convolution_bitcast_fusion.6
  139.1 1.7 convolution_bitcast_fusion.5
  142.6 1.7 convolution_bitcast_fusion.5
  146.2 1.7 convolution_bitcast_fusion.5
  148.0 1.7 convolution_bitcast_fusion.6
  149.7 1.7 convolution_bitcast_fusion.5
  153.3 1.7 convolution_bitcast_fusion.5
  156.8 1.7 convolution_bitcast_fusion.5
  158.6 1.7 convolution_bitcast_fusion.6
  160.3 1.7 convolution_bitcast_fusion.5
  163.9 1.7 convolution_bitcast_fusion.5
  167.4 1.7 convolution_bitcast_fusion.5
  169.3 1.7 convolution_bitcast_fusion.6
  171.0 1.7 convolution_bitcast_fusion.5
  174.5 1.7 convolution_bitcast_fusion.5
  178.1 1.7 convolution_bitcast_fusion.5
  179.9 1.7 convolution_bitcast_fusion.6
  181.6 1.7 convolution_bitcast_fusion.5
  185.1 1.7 convolution_bitcast_fusion.5
  188.7 1.7 convolution_bitcast_fusion.5
  190.5 1.7 convolution_bitcast_fusion.6
  192.2 1.7 convolution_bitcast_fusion.5
  195.8 1.7 convolution_bitcast_fusion.5
  199.3 1.7 convolution_bitcast_fusion.5
  201.2 1.7 convolution_bitcast_fusion.6
  202.9 1.7 convolution_bitcast_fusion.5
  206.4 1.7 convolution_bitcast_fusion.5
  209.9 1.7 convolution_bitcast_fusion.5
  213.5 1.7 convolution_bitcast_fusion.5
  217.0 1.7 convolution_bitcast_fusion.5
  220.6 1.7 convolution_bitcast_fusion.5
  224.1 1.7 convolution_bitcast_fusion.5
  227.7 1.7 convolution_bitcast_fusion.5
  231.2 1.7 convolution_bitcast_fusion.5
  233.0 1.7 convolution_bitcast_fusion.6
  234.7 1.7 convolution_bitcast_fusion.5
  239.0 11.7 %cholesky.172 = f32[128,128]{1,0:T(8,128)S(1)} custom-call(f32[128,128]{1,0:T(8,128)S(1)} %cholesky.270), custom_call_target="Cholesky" | custom-call | tf_op jit(solution)/shard_map/jit(cholesky)/cholesky | solution.py:60
  250.7 9.8 %custom-call.20 = f32[1,128,128]{1,2,0:T(8,128)S(1)} custom-call(f32[1,128,128]{2,1,0:T(8,128)S(1)} %get-tuple-element.157), custom_call_target="InvertDiagBlocksLowerTriangular" | custom-call | tf_op jit(solution)/shard_map/jit(cholesky)/cholesky | solution.py:60
  261.0 11.7 %cholesky.189 = f32[128,128]{1,0:T(8,128)S(1)} custom-call(f32[128,128]{1,0:T(8,128)S(1)} %convolution_subtract_fusion.3), custom_call_target="Cholesky" | custom-call | tf_op jit(solution)/shard_map/jit(cholesky)/cholesky | solution.py:60
  275.2 4.2 while.16
  279.5 19.8 %custom-call.15 = f32[2,128,128]{1,2,0:T(8,128)S(1)} custom-call(f32[2,128,128]{2,1,0:T(8,128)S(1)} %get-tuple-element.47), custom_call_target="InvertDiagBlocksLowerTriangular" | custom-call | tf_op jit(solution)/shard_map/jit(_solve_triangular)/triangular_solve | solution.py:63
  300.7 2.2 collective-permute-start
  306.7 11.7 %cholesky.206 = f32[128,128]{1,0:T(8,128)S(1)} custom-call(f32[128,128]{1,0:T(8,128)S(1)} %cholesky.273), custom_call_target="Cholesky" | custom-call | tf_op jit(solution)/shard_map/jit(cholesky)/cholesky | solution.py:60
  318.4 9.8 %custom-call.21 = f32[1,128,128]{1,2,0:T(8,128)S(1)} custom-call(f32[1,128,128]{2,1,0:T(8,128)S(1)} %get-tuple-element.155), custom_call_target="InvertDiagBlocksLowerTriangular" | custom-call | tf_op jit(solution)/shard_map/jit(cholesky)/cholesky | solution.py:60
  328.7 11.7 %cholesky.223 = f32[128,128]{1,0:T(8,128)S(1)} custom-call(f32[128,128]{1,0:T(8,128)S(1)} %convolution_subtract_fusion.2), custom_call_target="Cholesky" | custom-call | tf_op jit(solution)/shard_map/jit(cholesky)/cholesky | solution.py:60
  343.2 4.3 while.18
  347.6 19.7 %custom-call.22 = f32[2,128,128]{1,2,0:T(8,128)S(1)} custom-call(f32[2,128,128]{2,1,0:T(8,128)S(1)} %get-tuple-element.72), custom_call_target="InvertDiagBlocksLowerTriangular" | custom-call | tf_op jit(solution)/shard_map/jit(_solve_triangular)/triangular_solve | solution.py:63
  369.4 2.0 collective-permute-start.1
  372.6 6.3 %collective-permute-done.1 = f32[256,256]{0,1:T(8,128)S(1)} collective-permute-done((f32[256,256]{0,1:T(8,128)S(1)}, f32[256,256]{0,1:T(8,128)S(1)}, u32[]{:S(2)}, u32[]{:S(2)}) %collective-permute-start.1) | collective-permute-done | bytes 262176 | tf_op jit(solution)/shard_map/ppermute | solution.py:14
  381.5 11.7 %cholesky.240 = f32[128,128]{1,0:T(8,128)S(1)} custom-call(f32[128,128]{1,0:T(8,128)S(1)} %cholesky.276), custom_call_target="Cholesky" | custom-call | tf_op jit(solution)/shard_map/jit(cholesky)/cholesky | solution.py:60
  393.2 9.8 %custom-call.23 = f32[1,128,128]{1,2,0:T(8,128)S(1)} custom-call(f32[1,128,128]{2,1,0:T(8,128)S(1)} %get-tuple-element.151), custom_call_target="InvertDiagBlocksLowerTriangular" | custom-call | tf_op jit(solution)/shard_map/jit(cholesky)/cholesky | solution.py:60
  403.5 11.7 %cholesky.257 = f32[128,128]{1,0:T(8,128)S(1)} custom-call(f32[128,128]{1,0:T(8,128)S(1)} %convolution_subtract_fusion.1), custom_call_target="Cholesky" | custom-call | tf_op jit(solution)/shard_map/jit(cholesky)/cholesky | solution.py:60
  418.0 4.4 while.19
  422.4 19.7 %custom-call.24 = f32[2,128,128]{1,2,0:T(8,128)S(1)} custom-call(f32[2,128,128]{2,1,0:T(8,128)S(1)} %get-tuple-element.73), custom_call_target="InvertDiagBlocksLowerTriangular" | custom-call | tf_op jit(solution)/shard_map/jit(_solve_triangular)/triangular_solve | solution.py:63
  443.6 1.7 convolution_bitcast_fusion.2
  (248 shorter events, 72.7 us)
Async XLA Ops:
  7.2 74.2 %copy-start = (f32[3,1024]{1,0:T(4,128)S(1)}, f32[3,1024]{1,0:T(4,128)}, u32[]{:S(2)}) copy-start(f32[3,1024]{1,0:T(4,128)} %param.10) | copy-start | bytes 36868
  7.2 116.0 %all-gather.2.cloned.1.call-start = ((), (), s32[]{:S(2)}) async-start(), calls=%async_computation | async-start | bytes 4259840 | tf_op jit(solution)/shard_map/all_gather | solution.py:79
  300.7 3.4 collective-permute-start
  369.4 9.6 %collective-permute-start.1 = (f32[256,256]{0,1:T(8,128)S(1)}, f32[256,256]{0,1:T(8,128)S(1)}, u32[]{:S(2)}, u32[]{:S(2)}) collective-permute-start(f32[256,256]{0,1:T(8,128)S(1)} %fusion.30), channel_id=1, source_target_pairs={{0,16},{8,24},{16,0},{24,8},{32,48},{40,56},{48,32},{56,40},{64,80... | collective-permute-start | bytes 786440 | tf_op jit(solution)/shard_map/ppermute | solution.py:14
Sparse Core Ops, SparseCore 0:
  34.0 89.1 all-gather.1
where the time goes:
time: 457 us; the launch traced here: 453 us
  other arithmetic  167 us (37%)
  matrix products  121 us (26%)
  blocking collectives  72.1 us (16%)
  waiting for transfers between devices  49.3 us (11%)
  between operations  22.2 us (5%)
  local copies, waits for them, and re-layouts  14.3 us (3%)
    another operation x20, other arithmetic, cholesky_basis(): jnp.linalg.cholesky(gram_matrix + shift_value * jnp.eye(nprobe_total, dty...  103 us
    another operation x7, other arithmetic, cholesky_basis(): return jax.scipy.linalg.solve_triangular(factor, matrix, lower=True)  59.3 us
    dot_general x32, matrix products, advance(): jnp.dot(probe_part, kernel_sin, preferred_element_type=jnp.float32)  54.3 us
    dot_general x32, matrix products, advance(): jnp.dot(probe_part, kernel_cos, preferred_element_type=jnp.float32)  54.1 us
    all_gather x1, blocking collectives, per_device(): lax.all_gather(sources, 'rows', axis=1, tiled=True)  46.2 us
    all_gather x1, waiting for transfers between devices, per_device(): lax.all_gather(all_probes, 'rows', axis=1, tiled=True)  41.8 us
    all_gather x1, blocking collectives, per_device(): all_probes = lax.all_gather(probes, 'probe', axis=0, tiled=True)  25.9 us
  transfers between devices with their start and end apart: 3, of which 3 were waited for; matrix products, arithmetic and copies ran while one was open for 0% of the time, Pallas kernels for 0%

commit v1 on v0

--- a/solution.py
+++ b/solution.py
@@ -76,7 +76,10 @@
     samples = adder(
         starting,
         (
-            lax.all_gather(all_probes, "rows", axis=1, tiled=True),
+            jnp.concatenate(
+                lax.all_to_all(jnp.stack([all_probes] * lax.axis_size("rows")), "rows", 0, 0),
+                axis=1,
+            ),
             lax.all_gather(sources, "rows", axis=1, tiled=True),
         ),
         jnp.int32(0),

time: 457 us -> 499 us (1.092)
  blocking collectives: 72.1 us -> 150 us
  waiting for transfers between devices: 49.3 us -> 7.75 us
  starting transfers between devices: 4.24 us -> 21.3 us
  between operations: 22.2 us -> 8.8 us
    all_gather x1, blocking collectives: 46.2 us -> 124 us  [per_device(): lax.all_gather(sources, 'rows', axis=1, tiled=True)]
    all_gather x1 -> x0, waiting for transfers between devices: 41.8 us -> none  [per_device(): lax.all_gather(all_probes, 'rows', axis=1, tiled=True)]
    all_to_all x0 -> x1, starting transfers between devices: none -> 17.1 us  [per_device(): lax.all_to_all(jnp.stack([all_probes] * lax.axis_size('rows')), 'rows', 0...]
  transfers between devices with their start and end apart: 3 -> 3, of which waited for: 3 -> 2; matrix products, arithmetic and copies ran while one was open for 0% -> 0% of each run, Pallas kernels for 0% -> 0%
where the time goes in v1:
time: 499 us; the launch traced here: 494 us
  other arithmetic  167 us (33%)
  blocking collectives  150 us (30%)
  matrix products  121 us (24%)
  starting transfers between devices  21.3 us (4%)
  local copies, waits for them, and re-layouts  16.2 us (3%)
  between operations  8.8 us (2%)
  waiting for transfers between devices  7.75 us (2%)
    all_gather x1, blocking collectives, per_device(): lax.all_gather(sources, 'rows', axis=1, tiled=True)  124 us
    another operation x20, other arithmetic, cholesky_basis(): jnp.linalg.cholesky(gram_matrix + shift_value * jnp.eye(nprobe_total, dty...  103 us
    another operation x7, other arithmetic, cholesky_basis(): return jax.scipy.linalg.solve_triangular(factor, matrix, lower=True)  59.3 us
    dot_general x32, matrix products, advance(): jnp.dot(probe_part, kernel_sin, preferred_element_type=jnp.float32)  54.2 us
    dot_general x32, matrix products, advance(): jnp.dot(probe_part, kernel_cos, preferred_element_type=jnp.float32)  54 us
    all_gather x1, blocking collectives, per_device(): all_probes = lax.all_gather(probes, 'probe', axis=0, tiled=True)  25.9 us
    all_to_all x1, starting transfers between devices, per_device(): lax.all_to_all(jnp.stack([all_probes] * lax.axis_size('rows')), 'rows', 0...  17.1 us
  transfers between devices with their start and end apart: 3, of which 2 were waited for; matrix products, arithmetic and copies ran while one was open for 0% of the time, Pallas kernels for 0%

profile of v1, /device:TPU:1, one launch (start us, length us, event | category | flops | bytes accessed | tf_op | source)
XLA Modules:
  0.0 494.1 jit_solution(17941880421391601033)
XLA Ops:
  0.6 25.9 %all_gather.6 = bf16[256,128]{1,0:T(8,128)(2,1)S(1)} all-gather(bf16[32,128]{1,0:T(8,128)(2,1)} %param.12), channel_id=1, replica_groups=mesh['rows'=64,'probe'=8] {'probe'}, dimensions={0}, use_global_device_ids=true | all-gather | bytes 73728 | tf_op jit(solution)/shard_map/all_gather | solution.py:73
  26.7 2.5 stack.8
  29.2 17.1 %all-to-all-start = ((bf16[64,256,128]{1,2,0:T(8,128)(2,1)}), bf16[64,256,128]{1,2,0:T(8,128)(2,1)}, u32[]{:S(2)}, u32[]{:S(2)}) async-start(bf16[64,256,128]{1,2,0:T(8,128)(2,1)} %stack.8), calls=%async_computation | async-start | bytes 8388608 | tf_op jit(solution)/shard_map/all_to_all | solution.py:80
  47.6 123.7 %all_gather.7 = bf16[3,8192]{1,0:T(4,128)(2,1)S(1)} all-gather(bf16[3,128]{1,0:T(4,128)(2,1)S(1)} %copy-done.1), channel_id=1, replica_groups=mesh['rows'=64,'probe'=8] {'rows'}, dimensions={1}, use_global_device_ids=true | all-gather | bytes 49920 | tf_op jit(solution)/shard_map/all_gather | solution.py:83
  171.4 113.8 %while.17 = (s32[]{:T(128)}, f32[2,256,128]{2,1,0:T(8,128)S(1)}, bf16[32,256,256]{1,2,0:T(8,128)(2,1)}, bf16[32,3,256]{2,1,0:T(4,128)(2,1)S(1)}, f32[3,128]{1,0:T(4,128)S(1)}, /*index=5*/s32[]{:T(128)}, s32[]{:T(128)}) while((s32[]{:T(128)}, f32[2,256,128]{2,1,0:T(8,128)S(1)}, bf16[32,256,256]{1,2,0:T(8,128)(2,1)}, ...), condition=%wide.region_1.2_spmd.clone, body=%wide.region_0.1_spmd.clone.sunk | while | flops 34669312 | bytes 1334875 | solution.py:45
  173.1 1.7 convolution_bitcast_fusion.5
  176.7 1.7 convolution_bitcast_fusion.5
  178.5 1.7 convolution_bitcast_fusion.6
  180.2 1.7 convolution_bitcast_fusion.5
  183.7 1.7 convolution_bitcast_fusion.5
  185.6 1.7 convolution_bitcast_fusion.6
  187.3 1.7 convolution_bitcast_fusion.5
  190.8 1.7 convolution_bitcast_fusion.5
  192.7 1.7 convolution_bitcast_fusion.6
  194.4 1.7 convolution_bitcast_fusion.5
  197.9 1.7 convolution_bitcast_fusion.5
  199.7 1.7 convolution_bitcast_fusion.6
  201.4 1.7 convolution_bitcast_fusion.5
  205.0 1.7 convolution_bitcast_fusion.5
  206.8 1.7 convolution_bitcast_fusion.6
  208.5 1.7 convolution_bitcast_fusion.5
  212.1 1.7 convolution_bitcast_fusion.5
  213.9 1.7 convolution_bitcast_fusion.6
  215.6 1.7 convolution_bitcast_fusion.5
  219.1 1.7 convolution_bitcast_fusion.5
  222.7 1.7 convolution_bitcast_fusion.5
  226.2 1.7 convolution_bitcast_fusion.5
  228.1 1.7 convolution_bitcast_fusion.6
  229.8 1.7 convolution_bitcast_fusion.5
  233.3 1.7 convolution_bitcast_fusion.5
  236.9 1.7 convolution_bitcast_fusion.5
  240.4 1.7 convolution_bitcast_fusion.5
  243.9 1.7 convolution_bitcast_fusion.5
  247.5 1.7 convolution_bitcast_fusion.5
  251.0 1.7 convolution_bitcast_fusion.5
  254.6 1.7 convolution_bitcast_fusion.5
  256.4 1.7 convolution_bitcast_fusion.6
  258.1 1.7 convolution_bitcast_fusion.5
  261.6 1.7 convolution_bitcast_fusion.5
  265.2 1.7 convolution_bitcast_fusion.5
  268.7 1.7 convolution_bitcast_fusion.5
  272.3 1.7 convolution_bitcast_fusion.5
  275.8 1.7 convolution_bitcast_fusion.5
  279.3 1.7 convolution_bitcast_fusion.5
  282.9 1.7 convolution_bitcast_fusion.5
  287.1 11.7 %cholesky.172 = f32[128,128]{1,0:T(8,128)S(1)} custom-call(f32[128,128]{1,0:T(8,128)S(1)} %cholesky.270), custom_call_target="Cholesky" | custom-call | tf_op jit(solution)/shard_map/jit(cholesky)/cholesky | solution.py:60
  298.9 9.8 %custom-call.20 = f32[1,128,128]{1,2,0:T(8,128)S(1)} custom-call(f32[1,128,128]{2,1,0:T(8,128)S(1)} %get-tuple-element.148), custom_call_target="InvertDiagBlocksLowerTriangular" | custom-call | tf_op jit(solution)/shard_map/jit(cholesky)/cholesky | solution.py:60
  309.2 11.7 %cholesky.189 = f32[128,128]{1,0:T(8,128)S(1)} custom-call(f32[128,128]{1,0:T(8,128)S(1)} %convolution_subtract_fusion.3), custom_call_target="Cholesky" | custom-call | tf_op jit(solution)/shard_map/jit(cholesky)/cholesky | solution.py:60
  323.5 4.3 while.16
  327.8 19.8 %custom-call.15 = f32[2,128,128]{1,2,0:T(8,128)S(1)} custom-call(f32[2,128,128]{2,1,0:T(8,128)S(1)} %get-tuple-element.47), custom_call_target="InvertDiagBlocksLowerTriangular" | custom-call | tf_op jit(solution)/shard_map/jit(_solve_triangular)/triangular_solve | solution.py:63
  349.1 1.9 collective-permute-start
  355.2 11.7 %cholesky.206 = f32[128,128]{1,0:T(8,128)S(1)} custom-call(f32[128,128]{1,0:T(8,128)S(1)} %cholesky.273), custom_call_target="Cholesky" | custom-call | tf_op jit(solution)/shard_map/jit(cholesky)/cholesky | solution.py:60
  366.9 9.8 %custom-call.21 = f32[1,128,128]{1,2,0:T(8,128)S(1)} custom-call(f32[1,128,128]{2,1,0:T(8,128)S(1)} %get-tuple-element.146), custom_call_target="InvertDiagBlocksLowerTriangular" | custom-call | tf_op jit(solution)/shard_map/jit(cholesky)/cholesky | solution.py:60
  377.2 11.7 %cholesky.223 = f32[128,128]{1,0:T(8,128)S(1)} custom-call(f32[128,128]{1,0:T(8,128)S(1)} %convolution_subtract_fusion.2), custom_call_target="Cholesky" | custom-call | tf_op jit(solution)/shard_map/jit(cholesky)/cholesky | solution.py:60
  391.6 4.3 while.18
  395.9 19.7 %custom-call.22 = f32[2,128,128]{1,2,0:T(8,128)S(1)} custom-call(f32[2,128,128]{2,1,0:T(8,128)S(1)} %get-tuple-element.72), custom_call_target="InvertDiagBlocksLowerTriangular" | custom-call | tf_op jit(solution)/shard_map/jit(_solve_triangular)/triangular_solve | solution.py:63
  417.7 2.2 collective-permute-start.1
  421.1 6.3 %collective-permute-done.1 = f32[256,256]{0,1:T(8,128)S(1)} collective-permute-done((f32[256,256]{0,1:T(8,128)S(1)}, f32[256,256]{0,1:T(8,128)S(1)}, u32[]{:S(2)}, u32[]{:S(2)}) %collective-permute-start.1) | collective-permute-done | bytes 262176 | tf_op jit(solution)/shard_map/ppermute | solution.py:14
  430.0 11.7 %cholesky.240 = f32[128,128]{1,0:T(8,128)S(1)} custom-call(f32[128,128]{1,0:T(8,128)S(1)} %cholesky.276), custom_call_target="Cholesky" | custom-call | tf_op jit(solution)/shard_map/jit(cholesky)/cholesky | solution.py:60
  441.8 9.8 %custom-call.23 = f32[1,128,128]{1,2,0:T(8,128)S(1)} custom-call(f32[1,128,128]{2,1,0:T(8,128)S(1)} %get-tuple-element.142), custom_call_target="InvertDiagBlocksLowerTriangular" | custom-call | tf_op jit(solution)/shard_map/jit(cholesky)/cholesky | solution.py:60
  452.1 11.7 %cholesky.257 = f32[128,128]{1,0:T(8,128)S(1)} custom-call(f32[128,128]{1,0:T(8,128)S(1)} %convolution_subtract_fusion.1), custom_call_target="Cholesky" | custom-call | tf_op jit(solution)/shard_map/jit(cholesky)/cholesky | solution.py:60
  466.5 4.3 while.19
  470.8 19.7 %custom-call.24 = f32[2,128,128]{1,2,0:T(8,128)S(1)} custom-call(f32[2,128,128]{2,1,0:T(8,128)S(1)} %get-tuple-element.73), custom_call_target="InvertDiagBlocksLowerTriangular" | custom-call | tf_op jit(solution)/shard_map/jit(_solve_triangular)/triangular_solve | solution.py:63
  492.0 1.7 convolution_bitcast_fusion.2
  (250 shorter events, 74.1 us)
Async XLA Ops:
  0.6 170.7 %copy-start = (f32[3,1024]{1,0:T(4,128)S(1)}, f32[3,1024]{1,0:T(4,128)}, u32[]{:S(2)}) copy-start(f32[3,1024]{1,0:T(4,128)} %param.10) | copy-start | bytes 36868
  29.2 18.5 %copy-start.1 = (bf16[3,128]{1,0:T(4,128)(2,1)S(1)}, bf16[3,128]{1,0:T(4,128)(2,1)}, u32[]{:S(2)}) copy-start(bf16[3,128]{1,0:T(4,128)(2,1)} %param.11) | copy-start | bytes 2308
  29.2 142.2 %all-to-all-start = ((bf16[64,256,128]{1,2,0:T(8,128)(2,1)}), bf16[64,256,128]{1,2,0:T(8,128)(2,1)}, u32[]{:S(2)}, u32[]{:S(2)}) async-start(bf16[64,256,128]{1,2,0:T(8,128)(2,1)} %stack.8), calls=%async_computation | async-start | bytes 8388608 | tf_op jit(solution)/shard_map/all_to_all | solution.py:80
  349.1 3.4 collective-permute-start
  417.7 9.7 %collective-permute-start.1 = (f32[256,256]{0,1:T(8,128)S(1)}, f32[256,256]{0,1:T(8,128)S(1)}, u32[]{:S(2)}, u32[]{:S(2)}) collective-permute-start(f32[256,256]{0,1:T(8,128)S(1)} %fusion.30), channel_id=1, source_target_pairs={{0,16},{8,24},{16,0},{24,8},{32,48},{40,56},{48,32},{56,40},{64,80... | collective-permute-start | bytes 786440 | tf_op jit(solution)/shard_map/ppermute | solution.py:14
